TPU v7x, 32 devices: a whole 2x2x4 slice. The times are simulated.
32 devices in a mesh: pipe: 4 (over y, core), expert: 4 (over z), tensor: 2 (over x).
Axes of the slice: x: 2, y: 2, z: 4, core: 2. Of those that a mesh axis runs over, the one named last changes fastest.
Arguments:
- acts: bfloat16 [4, 2, 512, 2048], P('pipe', None, 'expert', 'tensor'), may hold values from -6 to 6
- out_grad: bfloat16 [4, 2, 512, 2048], P('pipe', None, 'expert', 'tensor'), may hold values from -4 to 4
- probs: bfloat16 [4, 2, 512], P('pipe', None, 'expert'), may hold values from 0.099609375 to 1
- counts: int32 [4, 2, 4, 4], P('pipe', None, 'expert'), may hold values from 1 to 64, as said below
- w_gate: bfloat16 [4, 4, 1024, 512], P('pipe', 'expert', None, 'tensor'), may hold values from -0.125 to 0.125
- w_up: bfloat16 [4, 4, 1024, 512], P('pipe', 'expert', None, 'tensor'), may hold values from -0.125 to 0.125
- w_down: bfloat16 [4, 4, 512, 1024], P('pipe', 'expert', 'tensor'), may hold values from -0.25 to 0.25
Outputs:
- act_grad: bfloat16 [4, 2, 512, 2048], P('pipe', None, 'expert', 'tensor')
- prob_grad: bfloat16 [4, 2, 512], P('pipe', None, 'expert')
- gate_grad: bfloat16 [4, 4, 1024, 512], P('pipe', 'expert', None, 'tensor')
- up_grad: bfloat16 [4, 4, 1024, 512], P('pipe', 'expert', None, 'tensor')
- down_grad: bfloat16 [4, 4, 512, 1024], P('pipe', 'expert', 'tensor')
Inputs may be any that keep to these rules, and one draw needn't show every extreme that they name: Row [p, d, s] of counts sums to 128; for each section and direction one expert gets exactly 64 rows from every source; no count exceeds 64.
All inputs are finite; a program needn't handle non-finite values.
Results may differ from a plain program's by a relative error of at most 0.008.
Values may be sent and summed in bfloat16 or wider, within the bound.
A program may use at most 64 MiB of HBM per device.

v0:
```python
import jax
import jax.numpy as jnp
from jax import lax
from jax.sharding import PartitionSpec as P


def partner(array, axis, apart):
    return lax.ppermute(array, axis, [(i, i ^ 1 << apart) for i in range(lax.axis_size(axis))])


def silu_parts(gate):
    sigma = jax.nn.sigmoid(gate)
    return (gate * sigma, sigma * (1.0 + gate * (1.0 - sigma)))


def slot_tables(count_rows, slots):
    ends = jnp.cumsum(count_rows, axis=-1)
    starts = ends - count_rows
    position = jnp.arange(slots, dtype=jnp.int32)
    local = starts[..., None] + position
    live = position < count_rows[..., None]
    return (jnp.where(live, local, 0), live, starts, ends)


def global_slots(local, rows):
    dir_ids = jnp.arange(2, dtype=jnp.int32)[:, None, None]
    return (dir_ids * rows + local).reshape(-1)


def pack_rows(values, local, live):
    experts, slots = (local.shape[1], local.shape[2])
    rows, width = (values.shape[1], values.shape[2])
    taken = jnp.take(values.reshape(-1, width), global_slots(local, rows), axis=0)
    taken = jnp.where(live.reshape(-1)[:, None], taken, jnp.zeros_like(taken))
    return taken.reshape(2, experts, slots, width)


def pack_scalars(values, local, live):
    experts, slots = (local.shape[1], local.shape[2])
    rows = values.shape[1]
    taken = jnp.take(values.reshape(-1), global_slots(local, rows), axis=0)
    taken = jnp.where(live.reshape(-1), taken, jnp.zeros_like(taken))
    return taken.reshape(2, experts, slots)


def expert_terms(input_rows, grad_rows, prob_rows, full_gate, full_up, full_down):
    gate = jnp.dot(input_rows, full_gate, preferred_element_type=jnp.float32)
    up = jnp.dot(input_rows, full_up, preferred_element_type=jnp.float32)
    silu_value, slope = silu_parts(gate)
    act = (silu_value * up).astype(jnp.bfloat16)
    back = lax.dot_general(
        grad_rows, full_down, (((1,), (1,)), ((), ())), preferred_element_type=jnp.float32
    )
    prob_term = jnp.sum(act.astype(jnp.float32) * back, axis=1)
    scale = prob_rows.astype(jnp.float32)[:, None]
    d_gate = (scale * back * up * slope).astype(jnp.bfloat16)
    d_up = (scale * back * silu_value).astype(jnp.bfloat16)
    scaled = (scale * grad_rows.astype(jnp.float32)).astype(jnp.bfloat16)
    input_grad = lax.dot_general(
        d_gate, full_gate, (((1,), (1,)), ((), ())), preferred_element_type=jnp.float32
    )
    input_grad = input_grad + lax.dot_general(
        d_up, full_up, (((1,), (1,)), ((), ())), preferred_element_type=jnp.float32
    )
    gate_term = lax.dot_general(
        input_rows, d_gate, (((0,), (0,)), ((), ())), preferred_element_type=jnp.float32
    )
    up_term = lax.dot_general(
        input_rows, d_up, (((0,), (0,)), ((), ())), preferred_element_type=jnp.float32
    )
    down_term = lax.dot_general(
        act, scaled, (((0,), (0,)), ((), ())), preferred_element_type=jnp.float32
    )
    return (input_grad, prob_term, (gate_term, up_term, down_term))


def half_pair(first, whole, axis):
    half = whole.shape[axis] // 2
    lower = lax.slice_in_dim(whole, 0, half, axis=axis)
    higher = lax.slice_in_dim(whole, half, 2 * half, axis=axis)
    return (jnp.where(first, lower, higher), jnp.where(first, higher, lower))


def settle(keep, arrived):
    return (keep.astype(jnp.float32) + arrived.astype(jnp.float32)).astype(jnp.bfloat16)[None, None]


def on_device(acts, out_grad, probs, counts, w_gate, w_up, w_down):
    experts = lax.axis_size("expert")
    pipes = lax.axis_size("pipe")
    top_bit = pipes.bit_length() - 2
    rows = acts.shape[2]
    slots = 2 * rows // experts
    first = lax.axis_index("pipe") // (pipes // 2) == 0
    owned = (w_gate[0, 0], w_up[0, 0], w_down[0, 0])
    other = partner((owned[0], owned[1], owned[2]), "pipe", top_bit)
    full_gate = jnp.concatenate(
        [jnp.where(first, owned[0], other[0]), jnp.where(first, other[0], owned[0])], axis=0
    )
    full_up = jnp.concatenate(
        [jnp.where(first, owned[1], other[1]), jnp.where(first, other[1], owned[1])], axis=0
    )
    full_down = jnp.concatenate(
        [jnp.where(first, owned[2], other[2]), jnp.where(first, other[2], owned[2])], axis=1
    )
    local, live, starts, ends = slot_tables(counts[0, :, 0, :], slots)
    prob_slots = pack_scalars(probs[0], local, live)
    input_send = pack_rows(acts[0], local, live)
    grad_send = pack_rows(out_grad[0], local, live)
    input_half, grad_half, prob_recv = (
        lax.all_to_all(input_send, "expert", split_axis=1, concat_axis=1, tiled=True),
        lax.all_to_all(grad_send, "expert", split_axis=1, concat_axis=1, tiled=True),
        lax.all_to_all(prob_slots, "expert", split_axis=1, concat_axis=1, tiled=True),
    )
    input_recv, grad_recv = (
        lax.all_gather(input_half, "tensor", axis=3, tiled=True),
        lax.all_gather(grad_half, "tensor", axis=3, tiled=True),
    )
    width = input_recv.shape[-1]
    input_flat = input_recv.reshape(-1, width)
    grad_flat = grad_recv.reshape(-1, width)
    prob_flat = prob_recv.reshape(-1)
    input_grad, prob_term, weight_terms = expert_terms(
        input_flat, grad_flat, prob_flat, full_gate, full_up, full_down
    )
    row_part = lax.psum_scatter(input_grad, "tensor", scatter_dimension=1, tiled=True).astype(
        jnp.bfloat16
    )
    prob_sum = lax.psum(prob_term, "tensor").astype(jnp.bfloat16)
    half_width = row_part.shape[-1]
    back_rows, back_probs = (
        lax.all_to_all(
            row_part.reshape(2, experts, slots, half_width),
            "expert",
            split_axis=1,
            concat_axis=1,
            tiled=True,
        ),
        lax.all_to_all(
            prob_sum.reshape(2, experts, slots), "expert", split_axis=1, concat_axis=1, tiled=True
        ),
    )
    row_ids = jnp.arange(rows, dtype=jnp.int32)
    owner = jnp.sum((ends[:, None, :] <= row_ids[None, :, None]).astype(jnp.int32), axis=2)
    start_row = jnp.take_along_axis(starts, owner, axis=1)
    dir_ids = jnp.arange(2, dtype=jnp.int32)[:, None]
    slot_place = ((dir_ids * experts + owner) * slots + row_ids - start_row).reshape(-1)
    act_grad = jnp.take(back_rows.reshape(-1, half_width), slot_place, axis=0).reshape(
        1, 2, rows, half_width
    )
    prob_grad = jnp.take(back_probs.reshape(-1), slot_place, axis=0).reshape(1, 2, rows)
    gate_keep, gate_send = half_pair(first, weight_terms[0].astype(jnp.bfloat16), 0)
    up_keep, up_send = half_pair(first, weight_terms[1].astype(jnp.bfloat16), 0)
    down_keep, down_send = half_pair(first, weight_terms[2].astype(jnp.bfloat16), 1)
    arrived = partner((gate_send, up_send, down_send), "pipe", top_bit)
    return (
        act_grad,
        prob_grad,
        settle(gate_keep, arrived[0]),
        settle(up_keep, arrived[1]),
        settle(down_keep, arrived[2]),
    )


def solution(mesh):
    return jax.shard_map(
        on_device,
        mesh=mesh,
        in_specs=(
            P("pipe", None, "expert", "tensor"),
            P("pipe", None, "expert", "tensor"),
            P("pipe", None, "expert"),
            P("pipe", None, "expert", None),
            P("pipe", "expert", None, "tensor"),
            P("pipe", "expert", None, "tensor"),
            P("pipe", "expert", "tensor", None),
        ),
        out_specs=(
            P("pipe", None, "expert", "tensor"),
            P("pipe", None, "expert"),
            P("pipe", "expert", None, "tensor"),
            P("pipe", "expert", None, "tensor"),
            P("pipe", "expert", "tensor", None),
        ),
        check_vma=False,
    )
```

profile of v0, /device:TPU:8, one launch (start us, length us, event | category | flops | bytes accessed | tf_op | source)
XLA Modules:
  0.0 233.1 jit_solution(7988695467448487800)
XLA Ops:
  10.7 2.1 gather_fusion.5
  12.8 2.1 gather_fusion.4
  16.2 29.0 %all_to_all.25 = bf16[2,4,64,1024]{3,2,0,1:T(8,128)(2,1)S(1)} all-to-all(bf16[2,4,64,1024]{3,2,0,1:T(8,128)(2,1)S(1)} %copy.42), channel_id=1, replica_groups=mesh['pipe'=4,'expert'=4,'tensor'=2] {'expert'}, dimensions={1} | all-to-all | bytes 2097152 | tf_op jit(solution)/shard_map/all_to_all | solution.py:111
  47.9 5.3 %all-to-all-start.1 = ((bf16[2,4,64,1024]{3,2,0,1:T(8,128)(2,1)}), bf16[2,4,64,1024]{3,2,0,1:T(8,128)(2,1)S(1)}, u32[]{:S(2)}, u32[]{:S(2)}) async-start(bf16[2,4,64,1024]{3,2,0,1:T(8,128)(2,1)} %copy.40), calls=%async_computation.1 | async-start | bytes 2097152 | tf_op jit(solution)/shard_map/all_to_all | solution.py:112
  55.4 19.4 %all-to-all-done.1 = bf16[2,4,64,1024]{3,2,0,1:T(8,128)(2,1)S(1)} async-done(((bf16[2,4,64,1024]{3,2,0,1:T(8,128)(2,1)}), bf16[2,4,64,1024]{3,2,0,1:T(8,128)(2,1)S(1)}, u32[]{:S(2)}, u32[]{:S(2)}) %all-to-all-start.1) | async-done | bytes 1048608 | tf_op jit(solution)/shard_map/all_to_all | solution.py:112
  76.0 3.4 %gather_fusion = bf16[512]{0:T(512)(128)(2,1)S(1)} fusion(bf16[256]{0:T(256)(128)(2,1)S(1)} %bitcast.70, s32[1024]{0:T(1024)S(1)} %pad_clamp_fusion.2), kind=kCustom, calls=%fused_computation.2 | custom fusion | bytes 4096 | tf_op jit(solution)/shard_map/jit(_take)/gather | solution.py:41
  80.1 6.5 %all-to-all-start = ((bf16[2,4,64]{2,0,1:T(2,128)(2,1)}), bf16[2,4,64]{2,0,1:T(2,128)(2,1)S(1)}, u32[]{:S(2)}, u32[]{:S(2)}) async-start(bf16[2,4,64]{2,0,1:T(2,128)(2,1)} %copy.38), calls=%async_computation | async-start | bytes 4096 | tf_op jit(solution)/shard_map/all_to_all | solution.py:113
  88.1 2.5 %all-to-all-done = bf16[2,4,64]{2,0,1:T(2,128)(2,1)S(1)} async-done(((bf16[2,4,64]{2,0,1:T(2,128)(2,1)}), bf16[2,4,64]{2,0,1:T(2,128)(2,1)S(1)}, u32[]{:S(2)}, u32[]{:S(2)}) %all-to-all-start) | async-done | bytes 1056 | tf_op jit(solution)/shard_map/all_to_all | solution.py:113
  90.7 2.1 broadcast_select_fusion.8
  93.9 5.3 %collective-permute-done.2 = bf16[1024,256]{1,0:T(8,128)(2,1)} collective-permute-done((bf16[1024,256]{1,0:T(8,128)(2,1)S(1)}, bf16[1024,256]{1,0:T(8,128)(2,1)}, u32[]{:S(2)}, u32[]{:S(2)}) %collective-permute-start.2) | collective-permute-done | bytes 524320 | tf_op jit(solution)/shard_map/ppermute | solution.py:8
  100.4 3.3 %fusion.5 = f32[512,256]{0,1:T(8,128)} fusion(bf16[512,2048]{1,0:T(8,128)(2,1)} %bitcast.91, bf16[1024,256]{1,0:T(8,128)(2,1)S(1)} %get-tuple-element.15, bf16[1024,256]{1,0:T(8,128)(2,1)S(1)} %get-tuple-element.14), kind=kOutput, calls=%fused_computation.23 | convolution fusion | flops 538968064 | bytes 3670016 | tf_op jit(solution)/shard_map/dot_general | solution.py:47
  105.3 9.4 %all-gather.3.cloned.1.call-done = bf16[2,4,64,2048]{3,2,1,0:T(8,128)(2,1)} async-done(((bf16[2,4,64,1024]{3,2,1,0:T(8,128)(2,1)}), bf16[2,4,64,2048]{3,2,1,0:T(8,128)(2,1)}) %all-gather.3.cloned.1.call-update) | async-done | bytes 2097168 | tf_op jit(solution)/shard_map/all_gather | solution.py:117
  114.7 3.6 %multiply_reduce_fusion = (f32[512]{0:T(512)S(1)}, bf16[512,256]{0,1:T(8,128)(2,1)}, bf16[512,256]{0,1:T(8,128)(2,1)S(1)}, bf16[512,256]{0,1:T(8,128)(2,1)S(1)}) fusion(f32[512,256]{0,1:T(8,128)} %fusion.7, f32[512,256]{0,1:T(8,128)} %fusion.5, f32[512]{0:T(512)S(1)} %reshape.410, bf16[512,2048]{1,0:T(8,128)(2,1)} %bitcast.95, ...), kind=kOutput, calls=%fused_computation.29 | convolution fusion | flops 541457920 | bytes 4984832 | tf_op jit(solution)/shard_map/dot_general | solution.py:51
  119.1 2.7 %convolution_add_fusion = f32[512,2048]{1,0:T(8,128)} fusion(f32[512,2048]{1,0:T(8,128)S(1)} %fusion.6, bf16[512,256]{0,1:T(8,128)(2,1)S(1)} %get-tuple-element.10, bf16[1024,256]{1,0:T(8,128)(2,1)S(1)} %get-tuple-element.15, bf16[1024,256]{1,0:T(8,128)(2,1)S(1)} %get-tuple-element.14), kind=kOutput, calls=%fused_computation.7 | convolution fusion | flops 540016640 | bytes 9699328 | tf_op jit(solution)/shard_map/dot_general | solution.py:59
  122.0 2.4 %gather_fusion.3 = s32[256]{0:T(256)S(1)} fusion(s32[2,4]{1,0:T(2,128)S(1)} %sub.39, s32[256]{0:T(256)S(1)} %fusion.21), kind=kCustom, calls=%fused_computation.5 | custom fusion | bytes 4096 | tf_op jit(solution)/shard_map/jit(take_along_axis)/gather | solution.py:145
  124.6 4.9 %psum.7 = bf16[512]{0:T(512)(128)(2,1)S(1)} all-reduce(f32[512]{0:T(512)S(1)} %get-tuple-element.6), channel_id=1, replica_groups=mesh['pipe'=4,'expert'=4,'tensor'=2] {'tensor'}, use_global_device_ids=true, to_apply=%region_4.6 | all-reduce | flops 512 | bytes 3072 | tf_op jit(solution)/shard_map/psum | solution.py:129
  130.2 5.1 %all-to-all-start.4 = ((bf16[2,4,64]{2,0,1:T(2,128)(2,1)}), bf16[2,4,64]{2,0,1:T(2,128)(2,1)S(1)}, u32[]{:S(2)}, u32[]{:S(2)}) async-start(bf16[2,4,64]{2,0,1:T(2,128)(2,1)} %copy.46), calls=%async_computation.5 | async-start | bytes 4096 | tf_op jit(solution)/shard_map/all_to_all | solution.py:139
  135.4 2.5 %convolution_convert_fusion.2 = bf16[2048,256]{1,0:T(8,128)(2,1)S(1)} fusion(bf16[512,2048]{1,0:T(8,128)(2,1)} %bitcast.92, bf16[512,256]{0,1:T(8,128)(2,1)S(1)} %copy-done.9), kind=kOutput, calls=%fused_computation.10 | convolution fusion | flops 537395200 | bytes 3407872 | tf_op jit(solution)/shard_map/dot_general | solution.py:65
  140.5 35.9 %reduce-scatter.2.cloned.1.call-done = f32[512,1024]{1,0:T(8,128)} async-done(((f32[512,2048]{1,0:T(8,128)}), f32[512,1024]{1,0:T(8,128)}) %reduce-scatter.2.cloned.1.call-update) | async-done | bytes 2097168 | tf_op jit(solution)/shard_map/reduce_scatter | solution.py:126
  179.2 5.1 %all-to-all-start.3 = ((bf16[2,4,64,1024]{3,2,0,1:T(8,128)(2,1)}), bf16[2,4,64,1024]{3,2,0,1:T(8,128)(2,1)}, u32[]{:S(2)}, u32[]{:S(2)}) async-start(bf16[2,4,64,1024]{3,2,0,1:T(8,128)(2,1)} %copy.44), calls=%async_computation.4 | async-start | bytes 2097152 | tf_op jit(solution)/shard_map/all_to_all | solution.py:132
  194.2 7.3 %collective-permute-done.5 = bf16[256,1024]{1,0:T(8,128)(2,1)} collective-permute-done((bf16[256,1024]{1,0:T(8,128)(2,1)}, bf16[256,1024]{1,0:T(8,128)(2,1)}, u32[]{:S(2)}, u32[]{:S(2)}) %collective-permute-start.5) | collective-permute-done | bytes 524320 | tf_op jit(solution)/shard_map/ppermute | solution.py:8
  201.5 2.4 %fusion.10 = bf16[1,1,256,1024]{3,2,1,0:T(8,128)(2,1)} fusion(bf16[256,1024]{1,0:T(8,128)(2,1)} %collective-permute-done.5, pred[]{:T(512)S(6)} %eq.3, bf16[256,2048]{1,0:T(8,128)(2,1)} %convolution_convert_fusion), kind=kLoop, calls=%fused_computation.28 | loop fusion | flops 1310720 | bytes 2097153 | tf_op jit(solution)/shard_map/broadcast_in_dim | solution.py:85
  204.0 8.8 %collective-permute-done.3 = bf16[1024,256]{1,0:T(8,128)(2,1)} collective-permute-done((bf16[1024,256]{1,0:T(8,128)(2,1)}, bf16[1024,256]{1,0:T(8,128)(2,1)}, u32[]{:S(2)}, u32[]{:S(2)}) %collective-permute-start.3) | collective-permute-done | bytes 524320 | tf_op jit(solution)/shard_map/ppermute | solution.py:8
  214.8 7.3 %collective-permute-done.4 = bf16[1024,256]{1,0:T(8,128)(2,1)S(1)} collective-permute-done((bf16[1024,256]{1,0:T(8,128)(2,1)}, bf16[1024,256]{1,0:T(8,128)(2,1)S(1)}, u32[]{:S(2)}, u32[]{:S(2)}) %collective-permute-start.4) | collective-permute-done | bytes 524320 | tf_op jit(solution)/shard_map/ppermute | solution.py:8
  (101 shorter events, 40.5 us)
Async XLA Ops:
  7.2 3.5 %copy-start = (bf16[1,2,128,1024]{3,2,1,0:T(8,128)(2,1)S(1)}, bf16[1,2,128,1024]{3,2,1,0:T(8,128)(2,1)}, u32[]{:S(2)}) copy-start(bf16[1,2,128,1024]{3,2,1,0:T(8,128)(2,1)} %param.9) | copy-start | bytes 1572868
  7.2 93.2 %all-gather.5.cloned.1.call-start = ((), (), s32[]{:S(2)}) async-start(), calls=%async_computation.7 | async-start | bytes 3145728 | tf_op jit(solution)/shard_map/all_gather | solution.py:116
  46.8 6.4 %copy-start.4 = (bf16[1,1,256,1024]{3,2,1,0:T(8,128)(2,1)S(1)}, bf16[1,1,256,1024]{3,2,1,0:T(8,128)(2,1)}, u32[]{:S(2)}) copy-start(bf16[1,1,256,1024]{3,2,1,0:T(8,128)(2,1)} %param.15) | copy-start | bytes 1572868
  46.8 8.0 %copy-start.5 = (bf16[1,1,1024,256]{3,2,1,0:T(8,128)(2,1)S(1)}, bf16[1,1,1024,256]{3,2,1,0:T(8,128)(2,1)}, u32[]{:S(2)}) copy-start(bf16[1,1,1024,256]{3,2,1,0:T(8,128)(2,1)} %param.14) | copy-start | bytes 1572868
  47.9 26.9 %all-to-all-start.1 = ((bf16[2,4,64,1024]{3,2,0,1:T(8,128)(2,1)}), bf16[2,4,64,1024]{3,2,0,1:T(8,128)(2,1)S(1)}, u32[]{:S(2)}, u32[]{:S(2)}) async-start(bf16[2,4,64,1024]{3,2,0,1:T(8,128)(2,1)} %copy.40), calls=%async_computation.1 | async-start | bytes 2097152 | tf_op jit(solution)/shard_map/all_to_all | solution.py:112
  53.2 22.7 %copy-start.1 = (bf16[1,2,128]{2,1,0:T(2,128)(2,1)S(1)}, bf16[1,2,128]{2,1,0:T(2,128)(2,1)}, u32[]{:S(2)}) copy-start(bf16[1,2,128]{2,1,0:T(2,128)(2,1)} %param.11) | copy-start | bytes 1540
  53.2 61.5 %all-gather.3.cloned.1.call-start = ((), (), s32[]{:S(2)}) async-start(), calls=%async_computation.6 | async-start | bytes 3145728 | tf_op jit(solution)/shard_map/all_gather | solution.py:117
  53.2 37.4 %collective-permute-start = (bf16[256,1024]{1,0:T(8,128)(2,1)S(1)}, bf16[256,1024]{1,0:T(8,128)(2,1)}, u32[]{:S(2)}, u32[]{:S(2)}) collective-permute-start(bf16[256,1024]{1,0:T(8,128)(2,1)S(1)} %bitcast.77), channel_id=1, source_target_pairs={{0,16},{8,24},{16,0},{24,8},{1,17},{9,25},{17,1},{25,9},{2,18},{10... | collective-permute-start | bytes 1572872 | tf_op jit(solution)/shard_map/ppermute | solution.py:8
  54.8 38.0 %collective-permute-start.1 = (bf16[1024,256]{1,0:T(8,128)(2,1)S(1)}, bf16[1024,256]{1,0:T(8,128)(2,1)}, u32[]{:S(2)}, u32[]{:S(2)}) collective-permute-start(bf16[1024,256]{1,0:T(8,128)(2,1)S(1)} %bitcast.78), channel_id=1, source_target_pairs={{0,16},{8,24},{16,0},{24,8},{1,17},{9,25},{17,1},{25,9},{2,18},{10... | collective-permute-start | bytes 1572872 | tf_op jit(solution)/shard_map/ppermute | solution.py:8
  55.4 24.0 %copy-start.10 = (s32[1,2,1,4]{3,2,1,0:T(1,128)S(1)}, s32[1,2,1,4]{3,2,1,0:T(1,128)}, u32[]{:S(2)}) copy-start(s32[1,2,1,4]{3,2,1,0:T(1,128)} %param.12) | copy-start | bytes 100
  55.4 31.1 %copy-start.6 = (bf16[1,1,1024,256]{3,2,1,0:T(8,128)(2,1)S(1)}, bf16[1,1,1024,256]{3,2,1,0:T(8,128)(2,1)}, u32[]{:S(2)}) copy-start(bf16[1,1,1024,256]{3,2,1,0:T(8,128)(2,1)} %param.13) | copy-start | bytes 1572868
  80.1 10.5 %all-to-all-start = ((bf16[2,4,64]{2,0,1:T(2,128)(2,1)}), bf16[2,4,64]{2,0,1:T(2,128)(2,1)S(1)}, u32[]{:S(2)}, u32[]{:S(2)}) async-start(bf16[2,4,64]{2,0,1:T(2,128)(2,1)} %copy.38), calls=%async_computation | async-start | bytes 4096 | tf_op jit(solution)/shard_map/all_to_all | solution.py:113
  86.6 89.8 %reduce-scatter.2.cloned.1.call-start = ((), (), s32[]{:S(2)}) async-start(), calls=%async_computation.8 | async-start | bytes 6291456 | tf_op jit(solution)/shard_map/reduce_scatter | solution.py:126
  86.6 12.7 %collective-permute-start.2 = (bf16[1024,256]{1,0:T(8,128)(2,1)S(1)}, bf16[1024,256]{1,0:T(8,128)(2,1)}, u32[]{:S(2)}, u32[]{:S(2)}) collective-permute-start(bf16[1024,256]{1,0:T(8,128)(2,1)S(1)} %bitcast.79), channel_id=1, source_target_pairs={{0,16},{8,24},{16,0},{24,8},{1,17},{9,25},{17,1},{25,9},{2,18},{10... | collective-permute-start | bytes 1572872 | tf_op jit(solution)/shard_map/ppermute | solution.py:8
  100.4 3.3 %copy-start.11 = (bf16[2,4,64,2048]{3,2,1,0:T(8,128)(2,1)S(1)}, bf16[2,4,64,2048]{3,2,1,0:T(8,128)(2,1)}, u32[]{:S(2)}) copy-start(bf16[2,4,64,2048]{3,2,1,0:T(8,128)(2,1)} %all-gather.5.cloned.1.call-done) | copy-start | bytes 6291460
  103.7 11.0 %copy-start.7 = (bf16[256,1024]{1,0:T(8,128)(2,1)S(1)}, bf16[256,1024]{1,0:T(8,128)(2,1)}, u32[]{:S(2)}) copy-start(bf16[256,1024]{1,0:T(8,128)(2,1)} %get-tuple-element.16) | copy-start | bytes 1572868
  121.9 13.5 %copy-start.9 = (bf16[512,256]{0,1:T(8,128)(2,1)S(1)}, bf16[512,256]{0,1:T(8,128)(2,1)}, u32[]{:S(2)}) copy-start(bf16[512,256]{0,1:T(8,128)(2,1)} %copy-done.8) | copy-start | bytes 786436
  130.2 49.0 %all-to-all-start.4 = ((bf16[2,4,64]{2,0,1:T(2,128)(2,1)}), bf16[2,4,64]{2,0,1:T(2,128)(2,1)S(1)}, u32[]{:S(2)}, u32[]{:S(2)}) async-start(bf16[2,4,64]{2,0,1:T(2,128)(2,1)} %copy.46), calls=%async_computation.5 | async-start | bytes 4096 | tf_op jit(solution)/shard_map/all_to_all | solution.py:139
  135.3 2.5 %copy-start.13 = (bf16[2,4,64,2048]{3,2,1,0:T(8,128)(2,1)S(1)}, bf16[2,4,64,2048]{3,2,1,0:T(8,128)(2,1)}, u32[]{:S(2)}) copy-start(bf16[2,4,64,2048]{3,2,1,0:T(8,128)(2,1)} %all-gather.3.cloned.1.call-done) | copy-start | bytes 6291460
  135.4 2.5 %copy-start.14 = (bf16[512,256]{0,1:T(8,128)(2,1)S(1)}, bf16[512,256]{0,1:T(8,128)(2,1)}, u32[]{:S(2)}) copy-start(bf16[512,256]{0,1:T(8,128)(2,1)} %get-tuple-element.7) | copy-start | bytes 786436
  179.2 44.0 %all-to-all-start.3 = ((bf16[2,4,64,1024]{3,2,0,1:T(8,128)(2,1)}), bf16[2,4,64,1024]{3,2,0,1:T(8,128)(2,1)}, u32[]{:S(2)}, u32[]{:S(2)}) async-start(bf16[2,4,64,1024]{3,2,0,1:T(8,128)(2,1)} %copy.44), calls=%async_computation.4 | async-start | bytes 2097152 | tf_op jit(solution)/shard_map/all_to_all | solution.py:132
  186.4 15.2 %collective-permute-start.5 = (bf16[256,1024]{1,0:T(8,128)(2,1)}, bf16[256,1024]{1,0:T(8,128)(2,1)}, u32[]{:S(2)}, u32[]{:S(2)}) collective-permute-start(bf16[256,1024]{1,0:T(8,128)(2,1)} %broadcast_select_fusion.6), channel_id=1, source_target_pairs={{0,16},{8,24},{16,0},{24,8},{1,17},{9,25},{17,1},{25,9},{2,18},{10... | collective-permute-start | bytes 1572872 | tf_op jit(solution)/shard_map/ppermute | solution.py:8
  188.7 24.1 %collective-permute-start.3 = (bf16[1024,256]{1,0:T(8,128)(2,1)}, bf16[1024,256]{1,0:T(8,128)(2,1)}, u32[]{:S(2)}, u32[]{:S(2)}) collective-permute-start(bf16[1024,256]{1,0:T(8,128)(2,1)} %broadcast_select_fusion.1), channel_id=1, source_target_pairs={{0,16},{8,24},{16,0},{24,8},{1,17},{9,25},{17,1},{25,9},{2,18},{10... | collective-permute-start | bytes 1572872 | tf_op jit(solution)/shard_map/ppermute | solution.py:8
  190.1 32.1 %collective-permute-start.4 = (bf16[1024,256]{1,0:T(8,128)(2,1)}, bf16[1024,256]{1,0:T(8,128)(2,1)S(1)}, u32[]{:S(2)}, u32[]{:S(2)}) collective-permute-start(bf16[1024,256]{1,0:T(8,128)(2,1)} %broadcast_select_fusion), channel_id=1, source_target_pairs={{0,16},{8,24},{16,0},{24,8},{1,17},{9,25},{17,1},{25,9},{2,18},{10... | collective-permute-start | bytes 1572872 | tf_op jit(solution)/shard_map/ppermute | solution.py:8
  (4 other events, 6.3 us)
Sparse Core Ops, SparseCore 0:
  46.5 33.4 all-gather.4
  81.6 33.1 all-gather.2
  122.0 54.2 reduce-scatter.1
where the time goes:
time: 235 us; the launch traced here: 233 us
  waiting for transfers between devices  96.1 us (41%)
  blocking collectives  34 us (14%)
  starting transfers between devices  29.2 us (12%)
  other arithmetic  21.5 us (9%)
  local copies, waits for them, and re-layouts  21.3 us (9%)
  matrix products  17.1 us (7%)
  between operations  14 us (6%)
    reduce_scatter x1, waiting for transfers between devices, on_device(): lax.psum_scatter(input_grad, 'tensor', scatter_dimension=1, tiled=True)  35.9 us
    all_to_all x1, blocking collectives, on_device(): lax.all_to_all(input_send, 'expert', split_axis=1, concat_axis=1, tiled=T...  29 us
    ppermute x6, waiting for transfers between devices, partner(): lax.ppermute(array, axis, [(i, i ^ 1 << apart) for i in range(lax.axis_si...  28.8 us
    all_to_all x1, waiting for transfers between devices, on_device(): lax.all_to_all(grad_send, 'expert', split_axis=1, concat_axis=1, tiled=True)  19.4 us
    all_gather x1, waiting for transfers between devices, on_device(): lax.all_gather(grad_half, 'tensor', axis=3, tiled=True)  9.42 us
    ppermute x6, starting transfers between devices, partner(): lax.ppermute(array, axis, [(i, i ^ 1 << apart) for i in range(lax.axis_si...  7.15 us
    all_to_all x1, starting transfers between devices, on_device(): lax.all_to_all(prob_slots, 'expert', split_axis=1, concat_axis=1, tiled=T...  6.47 us
    broadcast_in_dim x3, other arithmetic, settle(): (keep.astype(jnp.float32) + arrived.astype(jnp.float32)).astype(jnp.bfloa...  5.44 us
  transfers between devices with their start and end apart: 13, of which 8 were waited for; matrix products, arithmetic and copies ran while one was open for 17% of the time, Pallas kernels for 0%

commit v1 on v0

v1 whole, which is shorter than its diff:
```python
import functools

import jax
import jax.numpy as jnp
from jax import lax
from jax.experimental import pallas as pl
from jax.experimental.pallas import tpu as pltpu
from jax.sharding import PartitionSpec as P

F32, BF16 = jnp.float32, jnp.bfloat16
MESH = pl.DeviceIdType.MESH


def mm(a, b, dims):
    return lax.dot_general(a, b, (dims, ((), ())), preferred_element_type=F32)


NN, NT, TN = ((1,), (0,)), ((1,), (1,)), ((0,), (0,))


def as_row(column):
    size = column.shape[0]
    eye = lax.broadcasted_iota(jnp.int32, (size, size), 0) == lax.broadcasted_iota(
        jnp.int32, (size, size), 1
    )
    return jnp.sum(jnp.where(eye, column, 0.0), axis=0, keepdims=True)


def as_column(row):
    size = row.shape[1]
    eye = lax.broadcasted_iota(jnp.int32, (size, size), 0) == lax.broadcasted_iota(
        jnp.int32, (size, size), 1
    )
    return jnp.sum(jnp.where(eye, row, 0.0), axis=1, keepdims=True)


def kernel(
    n,
    pipes,
    acts,
    grads,
    probs,
    counts,
    w_gate,
    w_up,
    w_down,
    act_out,
    prob_out,
    gate_out,
    up_out,
    down_out,
    pick,
    pack_x,
    pack_g,
    pack_p,
    xs,
    gs,
    ps,
    wg,
    wu,
    wd,
    dg,
    du,
    ac,
    sc,
    po,
    p_send,
    p_recv,
    q_send,
    q_recv,
    r_send,
    rq_send,
    ret,
    rq,
    dw_send,
    dd_send,
    dw_recv,
    dd_recv,
    send_z,
    recv_z,
    send_x,
    recv_x,
    send_y,
    recv_y,
    send_b,
    recv_b,
    local,
):
    me = lax.axis_index("expert")
    t = lax.axis_index("tensor")
    pipe = lax.axis_index("pipe")
    h = pipe // (pipes // 2)
    over_x = {"tensor": 1 - t}
    over_y = {"pipe": lax.rem(pipe + pipes // 2, pipes)}
    rows = acts.shape[1]
    slots = 2 * rows // n
    block = 2 * slots

    barrier = pltpu.get_barrier_semaphore()
    pl.semaphore_signal(barrier, inc=1, device_id=over_x, device_id_type=MESH)
    pl.semaphore_signal(barrier, inc=1, device_id=over_y, device_id_type=MESH)
    for k in range(1, n):
        pl.semaphore_signal(
            barrier, inc=1, device_id={"expert": lax.rem(me + k, n)}, device_id_type=MESH
        )

    own = [
        pltpu.make_async_copy(src, dst.at[h], local.at[i])
        for i, (src, dst) in enumerate(((w_gate, wg), (w_up, wu), (w_down, wd)))
    ]
    for copy in own:
        copy.start()
    pl.semaphore_wait(barrier, n + 1)
    weights = [
        pltpu.make_async_remote_copy(
            src, dst.at[h], send_y.at[i], recv_y.at[i], device_id=over_y, device_id_type=MESH
        )
        for i, (src, dst) in enumerate(((w_gate, wg), (w_up, wu), (w_down, wd)))
    ]
    for copy in weights:
        copy.start()

    def remote(src, dst, send, recv, where):
        return pltpu.make_async_remote_copy(
            src, dst, send, recv, device_id=where, device_id_type=MESH
        )

    all_x = acts[...].reshape(2 * rows, acts.shape[2])
    all_g = grads[...].reshape(2 * rows, grads.shape[2])
    all_p = jnp.concatenate([probs[0:1, :].astype(F32), probs[1:2, :].astype(F32)], axis=1)
    all_p = jnp.broadcast_to(all_p, (16, 2 * rows)).astype(BF16)
    slot = lax.broadcasted_iota(jnp.int32, (slots, 2 * rows), 0)
    lane = lax.broadcasted_iota(jnp.int32, (slots, 2 * rows), 1)
    starts = [jnp.int32(0), jnp.int32(0)]
    for e in range(n):
        for d in range(2):
            count = counts[d, e]
            hit = (lane == slot + (starts[d] + d * rows)) & (slot < count)
            pick[e, d * slots : (d + 1) * slots, :] = jnp.where(hit, 1.0, 0.0).astype(BF16)
            starts[d] = starts[d] + count

    def forward(s, which):
        buf = (xs, gs)[which]
        return remote(
            buf.at[t, s], buf.at[t, s], send_x.at[which, s], recv_x.at[which, s], over_x
        )

    def backward(s, which):
        src, dst = ((p_send, p_recv), (q_send, q_recv))[which]
        return remote(
            src.at[s], dst.at[s], send_x.at[2 + which, s], recv_x.at[2 + which, s], over_x
        )

    def to_expert(e, which):
        src, dst = (
            (pack_x.at[e], xs.at[t, me]),
            (pack_g.at[e], gs.at[t, me]),
            (pack_p.at[e], ps.at[me]),
        )[which]
        return remote(src, dst, send_z.at[which, e], recv_z.at[which, me], {"expert": e})

    def from_source(s, which):
        dst = (xs.at[t, s], gs.at[t, s], ps.at[s])[which]
        return remote(dst, dst, send_z.at[which, s], recv_z.at[which, s], {"expert": s})

    def to_source(s, which):
        src, dst = ((r_send.at[s], ret.at[me]), (rq_send.at[s], rq.at[me]))[which]
        return remote(src, dst, send_z.at[3 + which, s], recv_z.at[3 + which, me], {"expert": s})

    def from_expert(e, which):
        dst = (ret.at[e], rq.at[e])[which]
        return remote(dst, dst, send_z.at[3 + which, e], recv_z.at[3 + which, e], {"expert": e})

    order = [lax.rem(me + k, n) for k in range(n)]
    came = [lax.rem(me + n - k, n) for k in range(n)]
    xs[t, me] = mm(pick[me], all_x, NN).astype(BF16)
    forward(me, 0).start()
    for e in order[1:]:
        pack_x[e] = mm(pick[e], all_x, NN).astype(BF16)
        to_expert(e, 0).start()
    gs[t, me] = mm(pick[me], all_g, NN).astype(BF16)
    ps[me] = mm(all_p, pick[me], NT).astype(BF16)
    forward(me, 1).start()
    for e in order[1:]:
        pack_g[e] = mm(pick[e], all_g, NN).astype(BF16)
        to_expert(e, 1).start()
        pack_p[e] = mm(all_p, pick[e], NT).astype(BF16)
        to_expert(e, 2).start()

    for which in range(2):
        for s in came[1:]:
            from_source(s, which).wait_recv()
            forward(s, which).start()

    for copy in own:
        copy.wait()

    def settle_rows(s):
        backward(s, 0).wait_recv()
        backward(s, 1).wait_recv()
        total = po[s] + p_recv[s].astype(F32)
        prob = jnp.broadcast_to((q_send[s] + q_recv[s])[0:1], (16, block))
        return total.astype(BF16), prob.astype(BF16)

    def return_rows(s):
        total, prob = settle_rows(s)
        r_send[s] = total
        rq_send[s] = prob
        to_source(s, 0).start()
        to_source(s, 1).start()

    for at, s in enumerate(came):
        if at == 0:
            for copy in weights:
                copy.wait_recv()
        else:
            from_source(s, 2).wait_recv()
        other = (xs.at[1 - t, s], gs.at[1 - t, s])
        for which in range(2):
            remote(
                other[which], other[which], send_x.at[which, s], recv_x.at[which, s], over_x
            ).wait_recv()
        gate = mm(xs[0, s], wg[0], NN) + mm(xs[1, s], wg[1], NN)
        up = mm(xs[0, s], wu[0], NN) + mm(xs[1, s], wu[1], NN)
        back = mm(gs[0, s], wd[0], NT) + mm(gs[1, s], wd[1], NT)
        sigma = jax.nn.sigmoid(gate)
        silu = gate * sigma
        act = (silu * up).astype(BF16)
        ac[s] = act
        prob_term = jnp.sum(act.astype(F32) * back, axis=1, keepdims=True)
        scale = as_column(ps[s].astype(F32)[0:1])
        scaled = scale * back
        d_gate = (scaled * up * (sigma * (1.0 + gate * (1.0 - sigma)))).astype(BF16)
        d_up = (scaled * silu).astype(BF16)
        dg[s] = d_gate
        du[s] = d_up
        p_send[s] = (mm(d_gate, wg[1 - t], NT) + mm(d_up, wu[1 - t], NT)).astype(BF16)
        q_send[s] = jnp.broadcast_to(as_row(prob_term), (8, block))
        backward(s, 0).start()
        backward(s, 1).start()
        po[s] = mm(d_gate, wg[t], NT) + mm(d_up, wu[t], NT)
        sc[0, s] = (scale * gs[0, s].astype(F32)).astype(BF16)
        sc[1, s] = (scale * gs[1, s].astype(F32)).astype(BF16)
        if at >= 2:
            return_rows(came[at - 1])

    def terms(half, i):
        depth = n * block
        if i == 2:
            return mm(
                ac[...].reshape(depth, ac.shape[2]), sc[half].reshape(depth, sc.shape[3]), TN
            )
        d = (dg, du)[i]
        return mm(xs[half].reshape(depth, xs.shape[3]), d[...].reshape(depth, d.shape[2]), TN)

    partials = [
        remote(src, dst, send_b.at[i], recv_b.at[i], over_y)
        for i, (src, dst) in enumerate(
            (
                (dw_send.at[0], dw_recv.at[0]),
                (dw_send.at[1], dw_recv.at[1]),
                (dd_send, dd_recv),
            )
        )
    ]
    for i in range(2):
        dw_send[i] = terms(1 - h, i).astype(BF16)
        partials[i].start()
    dd_send[...] = terms(1 - h, 2).astype(BF16)
    partials[2].start()

    if n > 1:
        return_rows(came[n - 1])
    total, prob = settle_rows(me)
    ret[me] = total
    rq[me] = prob
    keep = [terms(h, i) for i in range(3)]
    partials[0].wait_recv()
    gate_out[...] = (keep[0] + dw_recv[0].astype(F32)).astype(BF16)

    for e in order[1:]:
        from_expert(e, 0).wait_recv()
        from_expert(e, 1).wait_recv()
    chosen = pick[...].reshape(n * block, 2 * rows)
    back_rows = mm(chosen, ret[...].reshape(n * block, ret.shape[2]), TN)
    act_out[...] = back_rows.astype(BF16).reshape(act_out.shape)
    back_prob = jnp.zeros((16, 2 * rows), F32)
    for e in range(n):
        back_prob = back_prob + mm(rq[e], pick[e], NN)
    prob_out[0:1, :] = back_prob[0:1, :rows].astype(BF16)
    prob_out[1:2, :] = back_prob[0:1, rows:].astype(BF16)

    partials[1].wait_recv()
    up_out[...] = (keep[1] + dw_recv[1].astype(F32)).astype(BF16)
    partials[2].wait_recv()
    down_out[...] = (keep[2] + dd_recv[...].astype(F32)).astype(BF16)

    for copy in weights + partials:
        copy.wait_send()
    for s in came:
        for which in range(2):
            forward(s, which).wait_send()
            backward(s, which).wait_send()
    for e in order[1:]:
        for which in range(3):
            to_expert(e, which).wait_send()
        for which in range(2):
            to_source(e, which).wait_send()


def on_device(acts, out_grad, probs, counts, w_gate, w_up, w_down):
    n = lax.axis_size("expert")
    pipes = lax.axis_size("pipe")
    rows, width = acts.shape[2], acts.shape[3]
    slots = 2 * rows // n
    block = 2 * slots
    deep, hidden = w_gate.shape[2], w_gate.shape[3]
    v = pltpu.VMEM
    dma = pltpu.SemaphoreType.DMA
    vmem = pl.BlockSpec(memory_space=pltpu.VMEM)
    hbm = pl.BlockSpec(memory_space=pl.ANY)
    outs = pl.pallas_call(
        functools.partial(kernel, n, pipes),
        out_shape=(
            jax.ShapeDtypeStruct((2, rows, width), BF16),
            jax.ShapeDtypeStruct((2, rows), BF16),
            jax.ShapeDtypeStruct((deep, hidden), BF16),
            jax.ShapeDtypeStruct((deep, hidden), BF16),
            jax.ShapeDtypeStruct((hidden, deep), BF16),
        ),
        in_specs=[vmem, vmem, vmem, pl.BlockSpec(memory_space=pltpu.SMEM), hbm, hbm, hbm],
        out_specs=(vmem,) * 5,
        scratch_shapes=[
            v((n, block, 2 * rows), BF16),
            v((n, block, width), BF16),
            v((n, block, width), BF16),
            v((n, 16, block), BF16),
            v((2, n, block, width), BF16),
            v((2, n, block, width), BF16),
            v((n, 16, block), BF16),
            v((2, deep, hidden), BF16),
            v((2, deep, hidden), BF16),
            v((2, hidden, deep), BF16),
            v((n, block, hidden), BF16),
            v((n, block, hidden), BF16),
            v((n, block, hidden), BF16),
            v((2, n, block, width), BF16),
            v((n, block, width), F32),
            v((n, block, width), BF16),
            v((n, block, width), BF16),
            v((n, 8, block), F32),
            v((n, 8, block), F32),
            v((n, block, width), BF16),
            v((n, 16, block), BF16),
            v((n, block, width), BF16),
            v((n, 16, block), BF16),
            v((2, deep, hidden), BF16),
            v((hidden, deep), BF16),
            v((2, deep, hidden), BF16),
            v((hidden, deep), BF16),
            dma((5, n)),
            dma((5, n)),
            dma((4, n)),
            dma((4, n)),
            dma((3,)),
            dma((3,)),
            dma((3,)),
            dma((3,)),
            dma((3,)),
        ],
        compiler_params=pltpu.CompilerParams(
            collective_id=0, has_side_effects=True, vmem_limit_bytes=56 << 20
        ),
    )(acts[0], out_grad[0], probs[0], counts[0, :, 0, :], w_gate[0, 0], w_up[0, 0], w_down[0, 0])
    return (outs[0][None], outs[1][None]) + tuple(o[None, None] for o in outs[2:])


def solution(mesh):
    return jax.shard_map(
        on_device,
        mesh=mesh,
        in_specs=(
            P("pipe", None, "expert", "tensor"),
            P("pipe", None, "expert", "tensor"),
            P("pipe", None, "expert"),
            P("pipe", None, "expert", None),
            P("pipe", "expert", None, "tensor"),
            P("pipe", "expert", None, "tensor"),
            P("pipe", "expert", "tensor", None),
        ),
        out_specs=(
            P("pipe", None, "expert", "tensor"),
            P("pipe", None, "expert"),
            P("pipe", "expert", None, "tensor"),
            P("pipe", "expert", None, "tensor"),
            P("pipe", "expert", "tensor", None),
        ),
        check_vma=False,
    )
```

time: 235 us -> 127 us (0.54)
  Pallas kernels: 0 us -> 120 us
  waiting for transfers between devices: 96.1 us -> 0 us
  blocking collectives: 34 us -> 0 us
  starting transfers between devices: 29.2 us -> 0 us
  other arithmetic: 21.5 us -> 0 us
  matrix products: 17.1 us -> 0 us
  local copies, waits for them, and re-layouts: 21.3 us -> 5.7 us
  between operations: 14 us -> 0.66 us
    pallas_call x0 -> x1, Pallas kernels: none -> 120 us  [on_device(): pl.pallas_call(functools.partial(kernel, n, pipes), out_shape=(jax.ShapeD...]
    reduce_scatter x1 -> x0, waiting for transfers between devices: 35.9 us -> none  [on_device(): lax.psum_scatter(input_grad, 'tensor', scatter_dimension=1, tiled=True)]
    all_to_all x1 -> x0, blocking collectives: 29 us -> none  [on_device(): lax.all_to_all(input_send, 'expert', split_axis=1, concat_axis=1, tiled=T...]
    ppermute x6 -> x0, waiting for transfers between devices: 28.8 us -> none  [partner(): lax.ppermute(array, axis, [(i, i ^ 1 << apart) for i in range(lax.axis_si...]
    all_to_all x4 -> x0, starting transfers between devices: 22 us -> none  [the longest x1 6.47 us: on_device(): lax.all_to_all(prob_slots, 'expert', split_axis=1, concat_axis=1, tiled=T...]
    all_to_all x4 -> x0, waiting for transfers between devices: 21.9 us -> none  [the longest x1 19.4 us: on_device(): lax.all_to_all(grad_send, 'expert', split_axis=1, concat_axis=1, tiled=True)]
    dot_general x8 -> x0, matrix products: 17.1 us -> none  [the longest x1 3.64 us: expert_terms(): lax.dot_general(grad_rows, full_down, (((1,), (1,)), ((), ())), preferred...]
    gather x7 -> x0, local copies, waits for them, and re-layouts: 13.1 us -> none  [the longest x2 4.12 us: pack_rows(): jnp.take(values.reshape(-1, width), global_slots(local, rows), axis=0)]
  transfers between devices with their start and end apart: 13 -> 0, of which waited for: 8 -> 0; matrix products, arithmetic and copies ran while one was open for 17% -> 0% of each run, Pallas kernels for 0% -> 0%
where the time goes in v1:
time: 127 us
  Pallas kernels  120 us (94%)
  local copies, waits for them, and re-layouts  5.7 us (4%)
    pallas_call x1, Pallas kernels, on_device(): pl.pallas_call(functools.partial(kernel, n, pipes), out_shape=(jax.ShapeD...  120 us
    unnamed x13, local copies, waits for them, and re-layouts  5.7 us

profile of v1, /device:TPU:8, one launch (start us, length us, event | category | flops | bytes accessed | tf_op | source)
XLA Modules:
  0.0 126.7 jit_solution(4298990366147127867)
XLA Ops:
  0.6 120.3 %shard_map.110 = (bf16[2,128,1024]{2,1,0:T(8,128)(2,1)}, bf16[2,128]{1,0:T(2,128)(2,1)}, bf16[1024,256]{1,0:T(8,128)(2,1)}, bf16[1024,256]{1,0:T(8,128)(2,1)}, bf16[256,1024]{1,0:T(8,128)(2,1)}) custom-call(bf16[2,128,1024]{2,1,0:T(8,128)(2,1)} %bitcast.16, bf16[2,128,1024]{2,1,0:T(8,128)(2,1)} %bitcast.17, bf16[2,128]{1,0:T(2,128)(2,1)} %bitcast.22, ...), custom_call_target="tpu_custom_call" | custom-call | tf_op jit(solution)/shard_map/pallas_call | solution.py:322
  121.0 0.0 copy-start.3
  121.0 0.0 copy-start.2
  121.0 1.9 %copy.17 = bf16[1,2,128,1024]{3,2,1,0:T(8,128)(2,1)} copy(bf16[1,2,128,1024]{3,2,1,0:T(8,128)(2,1)} %bitcast.15) | data formatting | bytes 1048576
  122.9 0.0 copy-done.3
  122.9 0.5 copy.18
  123.4 0.0 copy-done.2
  123.4 0.0 copy-start.1
  123.4 0.8 copy.19
  124.2 0.4 copy-done.1
  124.7 0.0 copy-start
  124.7 0.8 copy.20
  125.4 0.4 copy-done
  125.9 0.8 copy.21
Async XLA Ops:
  121.0 1.9 %copy-start.3 = (bf16[2,128]{1,0:T(2,128)(2,1)S(1)}, bf16[2,128]{1,0:T(2,128)(2,1)}, u32[]{:S(2)}) copy-start(bf16[2,128]{1,0:T(2,128)(2,1)} %get-tuple-element.11) | copy-start | bytes 1540
  121.0 2.5 %copy-start.2 = (bf16[1024,256]{1,0:T(8,128)(2,1)S(1)}, bf16[1024,256]{1,0:T(8,128)(2,1)}, u32[]{:S(2)}) copy-start(bf16[1024,256]{1,0:T(8,128)(2,1)} %get-tuple-element.12) | copy-start | bytes 1572868
  123.4 1.2 copy-start.1
  124.7 1.2 copy-start

commit v2 on v1

--- a/solution.py
+++ b/solution.py
@@ -62,7 +62,11 @@
     dg,
     du,
     ac,
-    sc,
+    silus,
+    slopes,
+    acts_f,
+    sums,
+    sum_d,
     po,
     p_send,
     p_recv,
@@ -80,6 +84,8 @@
     recv_z,
     send_x,
     recv_x,
+    send_p,
+    recv_p,
     send_y,
     recv_y,
     send_b,
@@ -139,58 +145,61 @@
             pick[e, d * slots : (d + 1) * slots, :] = jnp.where(hit, 1.0, 0.0).astype(BF16)
             starts[d] = starts[d] + count
 
-    def forward(s, which):
-        buf = (xs, gs)[which]
-        return remote(
-            buf.at[t, s], buf.at[t, s], send_x.at[which, s], recv_x.at[which, s], over_x
-        )
+    def part(which):
+        return pl.ds(which % 2 * slots, slots)
+
+    def forward(s, which, half):
+        at = (xs, gs)[which // 2].at[half, s, part(which)]
+        return remote(at, at, send_x.at[which, s], recv_x.at[which, s], over_x)
 
     def backward(s, which):
         src, dst = ((p_send, p_recv), (q_send, q_recv))[which]
-        return remote(
-            src.at[s], dst.at[s], send_x.at[2 + which, s], recv_x.at[2 + which, s], over_x
-        )
+        return remote(src.at[s], dst.at[s], send_p.at[which, s], recv_p.at[which, s], over_x)
 
     def to_expert(e, which):
-        src, dst = (
-            (pack_x.at[e], xs.at[t, me]),
-            (pack_g.at[e], gs.at[t, me]),
-            (pack_p.at[e], ps.at[me]),
-        )[which]
+        if which == 4:
+            src, dst = pack_p.at[e], ps.at[me]
+        else:
+            pack, buf = ((pack_x, xs), (pack_g, gs))[which // 2]
+            src, dst = pack.at[e, part(which)], buf.at[t, me, part(which)]
         return remote(src, dst, send_z.at[which, e], recv_z.at[which, me], {"expert": e})
 
     def from_source(s, which):
-        dst = (xs.at[t, s], gs.at[t, s], ps.at[s])[which]
+        dst = ps.at[s] if which == 4 else (xs, gs)[which // 2].at[t, s, part(which)]
         return remote(dst, dst, send_z.at[which, s], recv_z.at[which, s], {"expert": s})
 
     def to_source(s, which):
         src, dst = ((r_send.at[s], ret.at[me]), (rq_send.at[s], rq.at[me]))[which]
-        return remote(src, dst, send_z.at[3 + which, s], recv_z.at[3 + which, me], {"expert": s})
+        return remote(src, dst, send_z.at[5 + which, s], recv_z.at[5 + which, me], {"expert": s})
 
     def from_expert(e, which):
         dst = (ret.at[e], rq.at[e])[which]
-        return remote(dst, dst, send_z.at[3 + which, e], recv_z.at[3 + which, e], {"expert": e})
+        return remote(dst, dst, send_z.at[5 + which, e], recv_z.at[5 + which, e], {"expert": e})
 
     order = [lax.rem(me + k, n) for k in range(n)]
     came = [lax.rem(me + n - k, n) for k in range(n)]
     xs[t, me] = mm(pick[me], all_x, NN).astype(BF16)
-    forward(me, 0).start()
+    for which in (0, 1):
+        forward(me, which, t).start()
     for e in order[1:]:
         pack_x[e] = mm(pick[e], all_x, NN).astype(BF16)
-        to_expert(e, 0).start()
+        for which in (0, 1):
+            to_expert(e, which).start()
     gs[t, me] = mm(pick[me], all_g, NN).astype(BF16)
     ps[me] = mm(all_p, pick[me], NT).astype(BF16)
-    forward(me, 1).start()
+    for which in (2, 3):
+        forward(me, which, t).start()
     for e in order[1:]:
         pack_g[e] = mm(pick[e], all_g, NN).astype(BF16)
-        to_expert(e, 1).start()
         pack_p[e] = mm(all_p, pick[e], NT).astype(BF16)
-        to_expert(e, 2).start()
-
-    for which in range(2):
+        for which in (2, 3, 4):
+            to_expert(e, which).start()
+
+    for whiches in ((0, 1), (2, 3)):
         for s in came[1:]:
-            from_source(s, which).wait_recv()
-            forward(s, which).start()
+            for which in whiches:
+                from_source(s, which).wait_recv()
+                forward(s, which, t).start()
 
     for copy in own:
         copy.wait()
@@ -209,49 +218,58 @@
         to_source(s, 0).start()
         to_source(s, 1).start()
 
-    for at, s in enumerate(came):
-        if at == 0:
-            for copy in weights:
-                copy.wait_recv()
-        else:
-            from_source(s, 2).wait_recv()
-        other = (xs.at[1 - t, s], gs.at[1 - t, s])
-        for which in range(2):
-            remote(
-                other[which], other[which], send_x.at[which, s], recv_x.at[which, s], over_x
-            ).wait_recv()
+    for copy in weights:
+        copy.wait_recv()
+    for s in came:
+        for which in (0, 1):
+            forward(s, which, 1 - t).wait_recv()
         gate = mm(xs[0, s], wg[0], NN) + mm(xs[1, s], wg[1], NN)
         up = mm(xs[0, s], wu[0], NN) + mm(xs[1, s], wu[1], NN)
-        back = mm(gs[0, s], wd[0], NT) + mm(gs[1, s], wd[1], NT)
         sigma = jax.nn.sigmoid(gate)
         silu = gate * sigma
-        act = (silu * up).astype(BF16)
-        ac[s] = act
-        prob_term = jnp.sum(act.astype(F32) * back, axis=1, keepdims=True)
-        scale = as_column(ps[s].astype(F32)[0:1])
-        scaled = scale * back
-        d_gate = (scaled * up * (sigma * (1.0 + gate * (1.0 - sigma)))).astype(BF16)
-        d_up = (scaled * silu).astype(BF16)
-        dg[s] = d_gate
-        du[s] = d_up
-        p_send[s] = (mm(d_gate, wg[1 - t], NT) + mm(d_up, wu[1 - t], NT)).astype(BF16)
-        q_send[s] = jnp.broadcast_to(as_row(prob_term), (8, block))
+        silus[s] = silu
+        slopes[s] = up * (sigma * (1.0 + gate * (1.0 - sigma)))
+        acts_f[s] = silu * up
+
+    def send_rows(s):
+        p_send[s] = (mm(dg[s], wg[1 - t], NT) + mm(du[s], wu[1 - t], NT)).astype(BF16)
         backward(s, 0).start()
         backward(s, 1).start()
-        po[s] = mm(d_gate, wg[t], NT) + mm(d_up, wu[t], NT)
-        sc[0, s] = (scale * gs[0, s].astype(F32)).astype(BF16)
-        sc[1, s] = (scale * gs[1, s].astype(F32)).astype(BF16)
+        po[s] = mm(dg[s], wg[t], NT) + mm(du[s], wu[t], NT)
+
+    def joined(ref, which):
+        return jnp.concatenate([ref[s] for s in which], axis=0)
+
+    def terms(half, i, which):
+        if i == 2:
+            return mm(joined(ac, which), joined(gs.at[half], which), TN)
+        return mm(joined(xs.at[half], which), joined((dg, du)[i], which), TN)
+
+    def later_rows(at):
+        send_rows(came[at])
         if at >= 2:
             return_rows(came[at - 1])
 
-    def terms(half, i):
-        depth = n * block
-        if i == 2:
-            return mm(
-                ac[...].reshape(depth, ac.shape[2]), sc[half].reshape(depth, sc.shape[3]), TN
-            )
-        d = (dg, du)[i]
-        return mm(xs[half].reshape(depth, xs.shape[3]), d[...].reshape(depth, d.shape[2]), TN)
+    for at, s in enumerate(came):
+        if at > 0:
+            from_source(s, 4).wait_recv()
+        for which in (2, 3):
+            forward(s, which, 1 - t).wait_recv()
+        back = mm(gs[0, s], wd[0], NT) + mm(gs[1, s], wd[1], NT)
+        act = acts_f[s]
+        prob_term = jnp.sum(act.astype(BF16).astype(F32) * back, axis=1, keepdims=True)
+        q_send[s] = jnp.broadcast_to(as_row(prob_term), (8, block))
+        scale = as_column(ps[s].astype(F32)[0:1])
+        ac[s] = (scale * act).astype(BF16)
+        scaled = scale * back
+        dg[s] = (scaled * slopes[s]).astype(BF16)
+        du[s] = (scaled * silus[s]).astype(BF16)
+        if at < n - 1:
+            later_rows(at)
+        if at == n - 2:
+            for i in range(2):
+                sums[i] = terms(1 - h, i, came[: n - 1])
+            sum_d[...] = terms(1 - h, 2, came[: n - 1])
 
     partials = [
         remote(src, dst, send_b.at[i], recv_b.at[i], over_y)
@@ -263,18 +281,19 @@
             )
         )
     ]
+    last = came[n - 1 :]
     for i in range(2):
-        dw_send[i] = terms(1 - h, i).astype(BF16)
+        dw_send[i] = (sums[i] + terms(1 - h, i, last)).astype(BF16)
         partials[i].start()
-    dd_send[...] = terms(1 - h, 2).astype(BF16)
+    dd_send[...] = (sum_d[...] + terms(1 - h, 2, last)).astype(BF16)
     partials[2].start()
-
-    if n > 1:
-        return_rows(came[n - 1])
+    later_rows(n - 1)
+
+    return_rows(came[n - 1])
     total, prob = settle_rows(me)
     ret[me] = total
     rq[me] = prob
-    keep = [terms(h, i) for i in range(3)]
+    keep = [terms(h, i, range(n)) for i in range(3)]
     partials[0].wait_recv()
     gate_out[...] = (keep[0] + dw_recv[0].astype(F32)).astype(BF16)
 
@@ -298,14 +317,23 @@
     for copy in weights + partials:
         copy.wait_send()
     for s in came:
+        for which in range(4):
+            forward(s, which, t).wait_send()
         for which in range(2):
-            forward(s, which).wait_send()
             backward(s, which).wait_send()
     for e in order[1:]:
-        for which in range(3):
+        for which in range(5):
             to_expert(e, which).wait_send()
         for which in range(2):
             to_source(e, which).wait_send()
+
+
+def hand_over(*refs):
+    copies = [pltpu.make_async_copy(refs[i], refs[5 + i], refs[10].at[i]) for i in range(5)]
+    for copy in copies:
+        copy.start()
+    for copy in copies:
+        copy.wait()
 
 
 def on_device(acts, out_grad, probs, counts, w_gate, w_up, w_down):
@@ -344,7 +372,11 @@
             v((n, block, hidden), BF16),
             v((n, block, hidden), BF16),
             v((n, block, hidden), BF16),
-            v((2, n, block, width), BF16),
+            v((n, block, hidden), F32),
+            v((n, block, hidden), F32),
+            v((n, block, hidden), F32),
+            v((2, deep, hidden), F32),
+            v((hidden, deep), F32),
             v((n, block, width), F32),
             v((n, block, width), BF16),
             v((n, block, width), BF16),
@@ -358,10 +390,12 @@
             v((hidden, deep), BF16),
             v((2, deep, hidden), BF16),
             v((hidden, deep), BF16),
-            dma((5, n)),
-            dma((5, n)),
+            dma((7, n)),
+            dma((7, n)),
             dma((4, n)),
             dma((4, n)),
+            dma((2, n)),
+            dma((2, n)),
             dma((3,)),
             dma((3,)),
             dma((3,)),
@@ -372,6 +406,13 @@
             collective_id=0, has_side_effects=True, vmem_limit_bytes=56 << 20
         ),
     )(acts[0], out_grad[0], probs[0], counts[0, :, 0, :], w_gate[0, 0], w_up[0, 0], w_down[0, 0])
+    outs = pl.pallas_call(
+        hand_over,
+        out_shape=[jax.ShapeDtypeStruct(o.shape, o.dtype) for o in outs],
+        in_specs=[vmem] * 5,
+        out_specs=[hbm] * 5,
+        scratch_shapes=[dma((5,))],
+    )(*outs)
     return (outs[0][None], outs[1][None]) + tuple(o[None, None] for o in outs[2:])
 
 

time: 127 us -> 117 us (0.921)
  local copies, waits for them, and re-layouts: 5.7 us -> 0 us
  Pallas kernels: 120 us -> 116 us
    pallas_call x1, Pallas kernels: 120 us -> 113 us  [on_device(): pl.pallas_call(functools.partial(kernel, n, pipes), out_shape=(jax.ShapeD...]
    unnamed x13 -> x0, local copies, waits for them, and re-layouts: 5.7 us -> none
    pallas_call x0 -> x1, Pallas kernels: none -> 2.88 us  [on_device(): pl.pallas_call(hand_over, out_shape=[jax.ShapeDtypeStruct(o.shape, o.dtyp...]
where the time goes in v2:
time: 117 us
  Pallas kernels  116 us (99%)
    pallas_call x1, Pallas kernels, on_device(): pl.pallas_call(functools.partial(kernel, n, pipes), out_shape=(jax.ShapeD...  113 us
    pallas_call x1, Pallas kernels, on_device(): pl.pallas_call(hand_over, out_shape=[jax.ShapeDtypeStruct(o.shape, o.dtyp...  2.88 us

profile of v2, /device:TPU:8, one launch (start us, length us, event | category | flops | bytes accessed | tf_op | source)
XLA Modules:
  0.0 117.0 jit_solution(15673396216398873836)
XLA Ops:
  0.6 113.5 %shard_map.110 = (bf16[2,128,1024]{2,1,0:T(8,128)(2,1)}, bf16[2,128]{1,0:T(2,128)(2,1)}, bf16[1024,256]{1,0:T(8,128)(2,1)}, bf16[1024,256]{1,0:T(8,128)(2,1)}, bf16[256,1024]{1,0:T(8,128)(2,1)}) custom-call(bf16[2,128,1024]{2,1,0:T(8,128)(2,1)} %bitcast.12, bf16[2,128,1024]{2,1,0:T(8,128)(2,1)} %bitcast.13, bf16[2,128]{1,0:T(2,128)(2,1)} %bitcast.18, ...), custom_call_target="tpu_custom_call" | custom-call | tf_op jit(solution)/shard_map/pallas_call | solution.py:350
  114.1 2.9 %shard_map.111 = (bf16[2,128,1024]{2,1,0:T(8,128)(2,1)}, bf16[2,128]{1,0:T(2,128)(2,1)}, bf16[1024,256]{1,0:T(8,128)(2,1)}, bf16[1024,256]{1,0:T(8,128)(2,1)}, bf16[256,1024]{1,0:T(8,128)(2,1)}) custom-call(bf16[2,128,1024]{2,1,0:T(8,128)(2,1)} %get-tuple-element.15.refs_0_, bf16[2,128]{1,0:T(2,128)(2,1)} %get-tuple-element.16.refs_1_, ...), custom_call_target="tpu_custom_call" | custom-call | tf_op jit(solution)/shard_map/pallas_call | solution.py:409

commit v3 on v2

--- a/solution.py
+++ b/solution.py
@@ -176,8 +176,9 @@
         dst = (ret.at[e], rq.at[e])[which]
         return remote(dst, dst, send_z.at[5 + which, e], recv_z.at[5 + which, e], {"expert": e})
 
-    order = [lax.rem(me + k, n) for k in range(n)]
-    came = [lax.rem(me + n - k, n) for k in range(n)]
+    turns = [0] + sorted(range(1, n), key=lambda k: -abs(2 * k - n))
+    order = [lax.rem(me + k, n) for k in turns]
+    came = [lax.rem(me + n - k, n) for k in turns]
     xs[t, me] = mm(pick[me], all_x, NN).astype(BF16)
     for which in (0, 1):
         forward(me, which, t).start()
@@ -245,11 +246,6 @@
             return mm(joined(ac, which), joined(gs.at[half], which), TN)
         return mm(joined(xs.at[half], which), joined((dg, du)[i], which), TN)
 
-    def later_rows(at):
-        send_rows(came[at])
-        if at >= 2:
-            return_rows(came[at - 1])
-
     for at, s in enumerate(came):
         if at > 0:
             from_source(s, 4).wait_recv()
@@ -265,7 +261,7 @@
         dg[s] = (scaled * slopes[s]).astype(BF16)
         du[s] = (scaled * silus[s]).astype(BF16)
         if at < n - 1:
-            later_rows(at)
+            send_rows(s)
         if at == n - 2:
             for i in range(2):
                 sums[i] = terms(1 - h, i, came[: n - 1])
@@ -287,9 +283,10 @@
         partials[i].start()
     dd_send[...] = (sum_d[...] + terms(1 - h, 2, last)).astype(BF16)
     partials[2].start()
-    later_rows(n - 1)
-
-    return_rows(came[n - 1])
+    send_rows(came[n - 1])
+
+    for s in came[1:]:
+        return_rows(s)
     total, prob = settle_rows(me)
     ret[me] = total
     rq[me] = prob

time: 117 us -> 108 us (0.923)
  the two profiles are of different devices: /device:TPU:8 before, /device:TPU:0 now
where the time goes in v3:
time: 108 us; the launch traced here: 107 us
  Pallas kernels  107 us (99%)
    pallas_call x1, Pallas kernels, on_device(): pl.pallas_call(functools.partial(kernel, n, pipes), out_shape=(jax.ShapeD...  104 us
    pallas_call x1, Pallas kernels, on_device(): pl.pallas_call(hand_over, out_shape=[jax.ShapeDtypeStruct(o.shape, o.dtyp...  2.88 us

profile of v3, /device:TPU:0, one launch (start us, length us, event | category | flops | bytes accessed | tf_op | source)
XLA Modules:
  0.0 107.4 jit_solution(9340549625487045510)
XLA Ops:
  0.6 103.9 %shard_map.110 = (bf16[2,128,1024]{2,1,0:T(8,128)(2,1)}, bf16[2,128]{1,0:T(2,128)(2,1)}, bf16[1024,256]{1,0:T(8,128)(2,1)}, bf16[1024,256]{1,0:T(8,128)(2,1)}, bf16[256,1024]{1,0:T(8,128)(2,1)}) custom-call(bf16[2,128,1024]{2,1,0:T(8,128)(2,1)} %bitcast.12, bf16[2,128,1024]{2,1,0:T(8,128)(2,1)} %bitcast.13, bf16[2,128]{1,0:T(2,128)(2,1)} %bitcast.18, ...), custom_call_target="tpu_custom_call" | custom-call | tf_op jit(solution)/shard_map/pallas_call | solution.py:347
  104.5 2.9 %shard_map.111 = (bf16[2,128,1024]{2,1,0:T(8,128)(2,1)}, bf16[2,128]{1,0:T(2,128)(2,1)}, bf16[1024,256]{1,0:T(8,128)(2,1)}, bf16[1024,256]{1,0:T(8,128)(2,1)}, bf16[256,1024]{1,0:T(8,128)(2,1)}) custom-call(bf16[2,128,1024]{2,1,0:T(8,128)(2,1)} %get-tuple-element.15.refs_0_, bf16[2,128]{1,0:T(2,128)(2,1)} %get-tuple-element.16.refs_1_, ...), custom_call_target="tpu_custom_call" | custom-call | tf_op jit(solution)/shard_map/pallas_call | solution.py:406
